TPU v7x, 32 devices: a whole 2x2x4 slice. The times are simulated.
32 devices in a mesh: occ: 8 (over y, x, core), sym: 4 (over z).
Axes of the slice: x: 2, y: 2, z: 4, core: 2. Of those that a mesh axis runs over, the one named last changes fastest.
Arguments:
- hole_part: bfloat16 [32, 8], replicated, may hold values from -768 to 768
- hole_block: float32 [32, 32], replicated, may hold values from -0.0078125 to 0.0078125
- amplitudes: bfloat16 [1280, 8, 4, 256], P(('occ', 'sym')), may hold values from -6 to 6
- pair_first: int32 [1280], P(('occ', 'sym')), may hold values from 0 to 31, as said below
- pair_block: int32 [1280], P(('occ', 'sym')), may hold values from 0 to 7, as said below
- occ_tiles: bfloat16 [32, 32, 1024], P('occ'), may hold values from -0.0048828125 to 0.0048828125
- vir_tiles: bfloat16 [1024, 32, 256], P(None, 'occ'), may hold values from -0.1875 to 0.1875
- occ_energy: float32 [32], replicated, may hold values from -2 to -0.5
- vir_energy: float32 [256], replicated, may hold values from 0.25 to 3
Outputs:
- sigma_pairs: bfloat16 [1280, 8, 4, 256], P(('occ', 'sym'))
- sigma_hole: float32 [32, 8], replicated
Inputs may be any that keep to these rules, and one draw needn't show every extreme that they name: `pair_first`: rows come in consecutive blocks of 40; in block b every value lies in [(b // 4) * 4, (b // 4) * 4 + 4). `pair_block`: rows come in consecutive blocks of 40; within one block no value is named by more than 5 rows. In every draw, for each s, all blocks b with b % 4 == s name one common value exactly 5 times.
All inputs are finite; a program needn't handle non-finite values.
Results may differ from a plain program's by a relative error of at most 0.0034.
Values may be sent and summed in bfloat16 or wider, within the bound.
A program may use at most 64 MiB of HBM per device.

v0:
```python
import jax
import jax.numpy as jnp
from jax import lax
from jax.sharding import PartitionSpec as P

CAP = 5


def body(
    hole_part,
    hole_block,
    amplitudes,
    pair_first,
    pair_block,
    occ_tiles,
    vir_tiles,
    occ_energy,
    vir_energy,
):
    highest = lax.Precision.HIGHEST
    groups = lax.axis_size("occ")
    own_group = lax.axis_index("occ")
    rows_here = amplitudes.shape[0]
    vectors = amplitudes.shape[1]
    block_occ = amplitudes.shape[2]
    virtuals = amplitudes.shape[3]
    auxiliary = vir_tiles.shape[0]
    columns = block_occ * virtuals
    slot_count = groups * CAP
    local_first = pair_first - own_group * block_occ
    first_hot = (local_first[:, None] == jnp.arange(block_occ, dtype=jnp.int32)[None, :]).astype(
        jnp.float32
    )
    dest_hot = (pair_block[:, None] == jnp.arange(groups, dtype=jnp.int32)[None, :]).astype(
        jnp.int32
    )
    earlier = jnp.cumsum(dest_hot, axis=0) - dest_hot
    rank_in = jnp.sum(earlier * dest_hot, axis=1)
    slot_of = pair_block * CAP + rank_in
    select = (jnp.arange(slot_count, dtype=jnp.int32)[:, None] == slot_of[None, :]).astype(
        jnp.bfloat16
    )
    slot_first = jnp.dot(select, first_hot.astype(jnp.bfloat16), preferred_element_type=jnp.float32)
    packed = jnp.dot(
        select, amplitudes.reshape(rows_here, vectors * columns), preferred_element_type=jnp.float32
    )
    packed = packed.astype(jnp.bfloat16).reshape(slot_count, vectors, columns)
    factors = jnp.einsum(
        "kv,ikq->ivq", hole_part, occ_tiles, preferred_element_type=jnp.float32
    ).astype(jnp.bfloat16)
    vir_flat = vir_tiles.reshape(auxiliary, columns)
    slot_factors = jnp.dot(
        slot_first.astype(jnp.bfloat16),
        factors.reshape(block_occ, vectors * auxiliary),
        preferred_element_type=jnp.float32,
    )
    slot_factors = slot_factors.astype(jnp.bfloat16).reshape(slot_count, vectors, auxiliary)
    got_amp, got_factors = (
        lax.all_to_all(packed, "occ", split_axis=0, concat_axis=0, tiled=True),
        lax.all_to_all(slot_factors, "occ", split_axis=0, concat_axis=0, tiled=True),
    )
    couple = jnp.dot(
        got_factors.reshape(slot_count * vectors, auxiliary),
        vir_flat,
        preferred_element_type=jnp.float32,
    )
    couple = couple.astype(jnp.bfloat16).reshape(slot_count, vectors, columns)
    partial_value = lax.dot_general(
        got_amp.reshape(slot_count * vectors, columns),
        vir_flat,
        (((1,), (1,)), ((), ())),
        preferred_element_type=jnp.float32,
    )
    partial_value = partial_value.reshape(slot_count, vectors, auxiliary)
    couple_home = lax.all_to_all(couple, "occ", split_axis=0, concat_axis=0, tiled=True)
    partial_home = lax.all_to_all(partial_value, "occ", split_axis=0, concat_axis=0, tiled=True)
    coupled_rows = jnp.dot(
        select.T,
        couple_home.reshape(slot_count, vectors * columns),
        preferred_element_type=jnp.float32,
    )
    coupled_rows = coupled_rows.reshape(rows_here, vectors, block_occ, virtuals)
    hole_terms = jnp.einsum("sl,svq->lvq", slot_first, partial_home, precision=highest)
    local_hole = jnp.einsum(
        "ikq,ivq->kv", occ_tiles.astype(jnp.float32), hole_terms, precision=highest
    )
    hole_total = lax.psum(local_hole, ("occ", "sym"))
    sigma_hole = hole_total + jnp.dot(hole_block, hole_part.astype(jnp.float32), precision=highest)
    own_energy = lax.dynamic_slice_in_dim(occ_energy, own_group * block_occ, block_occ, 0)
    first_energy = jnp.dot(first_hot, own_energy, precision=highest)
    second_index = pair_block[:, None] * block_occ + jnp.arange(block_occ, dtype=jnp.int32)[None, :]
    orbital_range = jnp.arange(occ_energy.shape[0], dtype=jnp.int32)
    second_energy = jnp.sum(
        jnp.where(
            second_index[:, :, None] == orbital_range[None, None, :], occ_energy[None, None, :], 0.0
        ),
        axis=-1,
    )
    shift = (
        vir_energy[None, None, None, :]
        - first_energy[:, None, None, None]
        - second_energy[:, None, :, None]
    )
    sigma_pairs = (coupled_rows + shift * amplitudes.astype(jnp.float32)).astype(jnp.bfloat16)
    return (sigma_pairs, sigma_hole)


def solution(mesh):
    placed = (
        P(),
        P(),
        P(("occ", "sym"), None, None, None),
        P(("occ", "sym")),
        P(("occ", "sym")),
        P("occ", None, None),
        P(None, "occ", None),
        P(),
        P(),
    )
    return jax.shard_map(
        body,
        mesh=mesh,
        in_specs=placed,
        out_specs=(P(("occ", "sym"), None, None, None), P()),
        check_vma=False,
    )
```

profile of v0, /device:TPU:0, one launch (start us, length us, event | category | flops | bytes accessed | tf_op | source)
XLA Modules:
  0.0 117.8 jit_solution(12540576212475311095)
XLA Ops:
  0.6 0.8 fusion.8
  1.5 0.8 select_reduce_fusion.1
  2.3 0.7 broadcast_multiply_fusion
  3.0 0.8 fusion.4
  3.9 0.7 broadcast_subtract_fusion.2
  4.6 0.2 fusion.10
  4.8 0.4 convolution_convert_fusion.1
  5.2 1.2 %copy.23 = bf16[5,8,8,1024]{3,2,1,0:T(8,128)(2,1)} copy(bf16[5,8,8,1024]{3,1,2,0:T(8,128)(2,1)S(1)} %bitcast.52) | data formatting | bytes 1310720
  6.4 5.2 %all-to-all-start = ((bf16[40,8,1024]{2,1,0:T(8,128)(2,1)}), bf16[40,8,1024]{2,1,0:T(8,128)(2,1)}, u32[]{:S(2)}, u32[]{:S(2)}) async-start(bf16[40,8,1024]{2,1,0:T(8,128)(2,1)} %bitcast.17), calls=%async_computation | async-start | bytes 1310720 | tf_op jit(solution)/shard_map/all_to_all | solution.py:60
  11.6 0.5 reshape.101
  12.1 0.5 convolution_convert_fusion
  12.5 1.2 %copy.26 = bf16[5,8,8,1024]{3,2,1,0:T(8,128)(2,1)} copy(bf16[5,8,8,1024]{3,1,2,0:T(8,128)(2,1)S(1)} %bitcast.53) | data formatting | bytes 1310720
  13.8 9.1 %all-to-all-done = bf16[40,8,1024]{2,1,0:T(8,128)(2,1)} async-done(((bf16[40,8,1024]{2,1,0:T(8,128)(2,1)}), bf16[40,8,1024]{2,1,0:T(8,128)(2,1)}, u32[]{:S(2)}, u32[]{:S(2)}) %all-to-all-start) | async-done | bytes 655392 | tf_op jit(solution)/shard_map/all_to_all | solution.py:60
  22.8 4.2 %all-to-all-start.2 = ((bf16[40,8,1024]{2,1,0:T(8,128)(2,1)}), bf16[40,8,1024]{2,1,0:T(8,128)(2,1)}, u32[]{:S(2)}, u32[]{:S(2)}) async-start(bf16[40,8,1024]{2,1,0:T(8,128)(2,1)} %bitcast.51), calls=%async_computation.2 | async-start | bytes 1310720 | tf_op jit(solution)/shard_map/all_to_all | solution.py:59
  27.1 0.5 copy.24
  27.6 2.8 %fusion.3 = bf16[40,8,1024]{2,1,0:T(8,128)(2,1)} fusion(bf16[1024,1024]{1,0:T(8,128)(2,1)S(1)} %bitcast.55, bf16[40,8,1024]{2,1,0:T(8,128)(2,1)} %all-to-all-done), kind=kOutput, calls=%fused_computation.7 | convolution fusion | flops 671416320 | bytes 3407872 | tf_op jit(solution)/shard_map/dot_general | solution.py:62
  30.3 7.9 %all-to-all-done.2 = bf16[40,8,1024]{2,1,0:T(8,128)(2,1)} async-done(((bf16[40,8,1024]{2,1,0:T(8,128)(2,1)}), bf16[40,8,1024]{2,1,0:T(8,128)(2,1)}, u32[]{:S(2)}, u32[]{:S(2)}) %all-to-all-start.2) | async-done | bytes 655392 | tf_op jit(solution)/shard_map/all_to_all | solution.py:59
  38.2 4.2 %all-to-all-start.1 = ((bf16[40,8,1024]{2,1,0:T(8,128)(2,1)}), bf16[40,8,1024]{2,1,0:T(8,128)(2,1)}, u32[]{:S(2)}, u32[]{:S(2)}) async-start(bf16[40,8,1024]{2,1,0:T(8,128)(2,1)} %fusion.3), calls=%async_computation.1 | async-start | bytes 1310720 | tf_op jit(solution)/shard_map/all_to_all | solution.py:75
  42.4 2.7 %reshape.107 = bf16[1024,1024,1]{1,0,2:T(8,128)(2,1)} reshape(bf16[1024,4,256]{2,1,0:T(4,128)(2,1)S(1)} %copy-done.1) | data formatting | bytes 4194304 | tf_op jit(solution)/shard_map/reshape | solution.py:51
  45.1 3.7 %fusion.20 = f32[40,8,1024]{2,1,0:T(8,128)} fusion(bf16[40,8,1024]{2,1,0:T(8,128)(2,1)} %all-to-all-done.2, bf16[1024,1024,1]{1,0,2:T(8,128)(2,1)} %reshape.107), kind=kOutput, calls=%fused_computation.41 | convolution fusion | flops 671088640 | bytes 4063232 | tf_op jit(solution)/shard_map/dot_general | solution.py:68
  48.9 4.7 %all-to-all-done.1 = bf16[40,8,1024]{2,1,0:T(8,128)(2,1)} async-done(((bf16[40,8,1024]{2,1,0:T(8,128)(2,1)}), bf16[40,8,1024]{2,1,0:T(8,128)(2,1)}, u32[]{:S(2)}, u32[]{:S(2)}) %all-to-all-start.1) | async-done | bytes 655392 | tf_op jit(solution)/shard_map/all_to_all | solution.py:75
  53.6 3.6 %all-to-all-start.3 = ((f32[40,8,1024]{2,1,0:T(8,128)}), f32[40,8,1024]{2,1,0:T(8,128)S(1)}, u32[]{:S(2)}, u32[]{:S(2)}) async-start(f32[40,8,1024]{2,1,0:T(8,128)} %fusion.20), calls=%async_computation.3 | async-start | bytes 2621440 | tf_op jit(solution)/shard_map/all_to_all | solution.py:76
  57.6 0.8 broadcast_subtract_fusion
  58.3 1.5 %copy.25 = bf16[5,8,8,1024]{3,1,2,0:T(8,128)(2,1)S(1)} copy(bf16[5,8,8,1024]{3,2,1,0:T(8,128)(2,1)} %bitcast.20) | data formatting | bytes 1310720
  59.8 0.5 dot_general.44
  60.3 1.8 %fusion = bf16[40,8,4,256]{3,0,2,1:T(8,128)(2,1)S(1)} fusion(bf16[40,8,4,256]{3,2,1,0:T(4,128)(2,1)S(1)} %copy-done.2, bf16[8,4,256,40]{2,1,0,3:T(4,128)(2,1)S(1)} %dot_general.44, f32[40,4,256]{2,0,1:T(8,128)} %broadcast_subtract_fusion, s32[40]{0:T(128)S(1)} %get-tuple-element.9), kind=kOutput, calls=%fused_computation.3 | convolution fusion | flops 27526720 | bytes 2130080 | tf_op jit(solution)/shard_map/dot_general | solution.py:77
  62.1 1.2 %copy.20 = bf16[40,8,4,256]{3,2,1,0:T(4,128)(2,1)} copy(bf16[40,8,4,256]{3,0,2,1:T(8,128)(2,1)S(1)} %fusion) | data formatting | bytes 1310720
  63.3 12.0 %all-to-all-done.3 = f32[40,8,1024]{2,1,0:T(8,128)S(1)} async-done(((f32[40,8,1024]{2,1,0:T(8,128)}), f32[40,8,1024]{2,1,0:T(8,128)S(1)}, u32[]{:S(2)}, u32[]{:S(2)}) %all-to-all-start.3) | async-done | bytes 1310752 | tf_op jit(solution)/shard_map/all_to_all | solution.py:76
  75.3 1.4 %fusion.1 = f32[4,8,1024]{2,0,1:T(4,128)S(1)} fusion(f32[40,8,1024]{2,1,0:T(8,128)S(1)} %all-to-all-done.3, f32[40,4]{0,1:T(4,128)S(1)} %fusion.10), kind=kOutput, calls=%fused_computation.5 | convolution fusion | flops 15728640 | bytes 1442432 | tf_op jit(solution)/shard_map/sl,svq->lvq/dot_general | solution.py:83
  76.7 0.3 convolution_bitcast_fusion
  77.1 39.9 %psum.7 = f32[32,8]{0,1:T(8,128)S(1)} all-reduce(f32[32,8]{0,1:T(8,128)S(1)} %convolution_bitcast_fusion), channel_id=1, replica_groups=mesh['occ'=8,'sym'=4] {'occ','sym'}, use_global_device_ids=true, to_apply=%region_3.4 | all-reduce | flops 256 | bytes 2048 | tf_op jit(solution)/shard_map/psum | solution.py:87
  117.0 0.7 convolution_add_fusion.1
  (20 shorter events, 0.5 us)
Async XLA Ops:
  0.6 2.4 %copy-start = (bf16[4,32,1024]{2,1,0:T(8,128)(2,1)S(1)}, bf16[4,32,1024]{2,1,0:T(8,128)(2,1)}, u32[]{:S(2)}) copy-start(bf16[4,32,1024]{2,1,0:T(8,128)(2,1)} %param.14) | copy-start | bytes 786436
  5.2 6.4 %copy-start.2 = (bf16[40,8,4,256]{3,2,1,0:T(4,128)(2,1)S(1)}, bf16[40,8,4,256]{3,2,1,0:T(4,128)(2,1)}, u32[]{:S(2)}) copy-start(bf16[40,8,4,256]{3,2,1,0:T(4,128)(2,1)} %param.11) | copy-start | bytes 1966084
  6.4 16.4 %all-to-all-start = ((bf16[40,8,1024]{2,1,0:T(8,128)(2,1)}), bf16[40,8,1024]{2,1,0:T(8,128)(2,1)}, u32[]{:S(2)}, u32[]{:S(2)}) async-start(bf16[40,8,1024]{2,1,0:T(8,128)(2,1)} %bitcast.17), calls=%async_computation | async-start | bytes 1310720 | tf_op jit(solution)/shard_map/all_to_all | solution.py:60
  12.5 14.5 %copy-start.1 = (bf16[1024,4,256]{2,1,0:T(4,128)(2,1)S(1)}, bf16[1024,4,256]{2,1,0:T(4,128)(2,1)}, u32[]{:S(2)}) copy-start(bf16[1024,4,256]{2,1,0:T(4,128)(2,1)} %param.15) | copy-start | bytes 6291460
  22.8 15.4 %all-to-all-start.2 = ((bf16[40,8,1024]{2,1,0:T(8,128)(2,1)}), bf16[40,8,1024]{2,1,0:T(8,128)(2,1)}, u32[]{:S(2)}, u32[]{:S(2)}) async-start(bf16[40,8,1024]{2,1,0:T(8,128)(2,1)} %bitcast.51), calls=%async_computation.2 | async-start | bytes 1310720 | tf_op jit(solution)/shard_map/all_to_all | solution.py:59
  38.2 15.4 %all-to-all-start.1 = ((bf16[40,8,1024]{2,1,0:T(8,128)(2,1)}), bf16[40,8,1024]{2,1,0:T(8,128)(2,1)}, u32[]{:S(2)}, u32[]{:S(2)}) async-start(bf16[40,8,1024]{2,1,0:T(8,128)(2,1)} %fusion.3), calls=%async_computation.1 | async-start | bytes 1310720 | tf_op jit(solution)/shard_map/all_to_all | solution.py:75
  48.9 8.3 %copy-start.6 = (f32[32]{0:T(128)S(1)}, f32[32]{0:T(128)}, u32[]{:S(2)}) copy-start(f32[32]{0:T(128)} %param.16) | copy-start | bytes 388
  48.9 8.6 %copy-start.5 = (f32[256]{0:T(256)S(1)}, f32[256]{0:T(256)}, u32[]{:S(2)}) copy-start(f32[256]{0:T(256)} %param.17) | copy-start | bytes 3076
  53.6 21.7 %all-to-all-start.3 = ((f32[40,8,1024]{2,1,0:T(8,128)}), f32[40,8,1024]{2,1,0:T(8,128)S(1)}, u32[]{:S(2)}, u32[]{:S(2)}) async-start(f32[40,8,1024]{2,1,0:T(8,128)} %fusion.20), calls=%async_computation.3 | async-start | bytes 2621440 | tf_op jit(solution)/shard_map/all_to_all | solution.py:76
  62.1 55.0 %copy-start.3 = (f32[32,32]{1,0:T(8,128)S(1)}, f32[32,32]{1,0:T(8,128)}, u32[]{:S(2)}) copy-start(f32[32,32]{1,0:T(8,128)} %param.10) | copy-start | bytes 12292
  62.1 55.0 %copy-start.4 = (bf16[32,8]{0,1:T(8,128)(2,1)S(1)}, bf16[32,8]{0,1:T(8,128)(2,1)}, u32[]{:S(2)}) copy-start(bf16[32,8]{0,1:T(8,128)(2,1)} %param.9) | copy-start | bytes 1540
where the time goes:
time: 118 us
  blocking collectives  39.9 us (34%)
  waiting for transfers between devices  33.7 us (29%)
  starting transfers between devices  17.1 us (14%)
  matrix products  13 us (11%)
  local copies, waits for them, and re-layouts  9.29 us (8%)
  other arithmetic  3.95 us (3%)
    psum x1, blocking collectives, body(): hole_total = lax.psum(local_hole, ('occ', 'sym'))  39.9 us
    all_to_all x1, waiting for transfers between devices, body(): lax.all_to_all(partial_value, 'occ', split_axis=0, concat_axis=0, tiled=T...  12 us
    all_to_all x1, waiting for transfers between devices, body(): lax.all_to_all(slot_factors, 'occ', split_axis=0, concat_axis=0, tiled=True)  9.09 us
    all_to_all x1, waiting for transfers between devices, body(): lax.all_to_all(packed, 'occ', split_axis=0, concat_axis=0, tiled=True)  7.87 us
    unnamed x20, local copies, waits for them, and re-layouts  5.64 us
    all_to_all x1, starting transfers between devices, body(): lax.all_to_all(slot_factors, 'occ', split_axis=0, concat_axis=0, tiled=True)  5.17 us
    all_to_all x1, waiting for transfers between devices, body(): lax.all_to_all(couple, 'occ', split_axis=0, concat_axis=0, tiled=True)  4.71 us
    all_to_all x1, starting transfers between devices, body(): lax.all_to_all(packed, 'occ', split_axis=0, concat_axis=0, tiled=True)  4.2 us
  transfers between devices with their start and end apart: 4, of which 4 were waited for; matrix products, arithmetic and copies ran while one was open for 15% of the time, Pallas kernels for 0%

commit v1 on v0

v1 whole, which is shorter than its diff:
```python
import functools

import jax
import jax.numpy as jnp
from jax import lax
from jax.experimental import pallas as pl
from jax.experimental.pallas import tpu as pltpu
from jax.sharding import PartitionSpec as P

MESH = pl.DeviceIdType.MESH
HIGHEST = lax.Precision.HIGHEST


def partner(me, step, count):
    if count & (count - 1):
        return lax.rem(me + step, count), lax.rem(me + count - step, count)
    other = me
    bit = 1
    while bit < count:
        if step & bit:
            other = other + bit * (1 - 2 * ((me // bit) % 2))
        bit *= 2
    return other, other


def kernel(
    n,
    ns,
    hole_ref,
    block_ref,
    x_ref,
    first_ref,
    dest_ref,
    occ_ref,
    vir_hbm,
    oe_ref,
    ve_ref,
    out_ref,
    hout_ref,
    vir,
    pick,
    pack,
    fac,
    got_a,
    got_f,
    cpl,
    cpl_home,
    back,
    back_home,
    red,
    red2,
    vsem,
    send_sem,
    recv_sem,
    zsend,
    zrecv,
):
    me = lax.axis_index("occ")
    own_z = lax.axis_index("sym")
    bo, no, aux = occ_ref.shape
    vec = hole_ref.shape[1]
    rows, cols = x_ref.shape
    virt = ve_ref.shape[1]
    pairs = first_ref.shape[1]
    part = bo * vec
    combos = n * part

    barrier = pltpu.get_barrier_semaphore()
    for j in range(1, n):
        pl.semaphore_signal(barrier, 1, device_id={"occ": partner(me, j, n)[0]}, device_id_type=MESH)
    for j in range(1, ns):
        pl.semaphore_signal(
            barrier, 1, device_id={"sym": partner(own_z, j, ns)[0]}, device_id_type=MESH
        )
    vcopy = pltpu.make_async_copy(vir_hbm, vir, vsem)
    vcopy.start()

    def rows_of(index):
        return pl.ds(pl.multiple_of(index * part, part), part)

    def copy_to(kind, j, src, dst):
        return pltpu.make_async_remote_copy(
            src_ref=src,
            dst_ref=dst,
            send_sem=send_sem.at[kind, j],
            recv_sem=recv_sem.at[kind, j],
            device_id={"occ": partner(me, j, n)[0]},
            device_id_type=MESH,
        )

    code = (dest_ref[...] * bo + first_ref[...] - me * bo).astype(jnp.float32)
    spread = (
        lax.broadcasted_iota(jnp.int32, (pairs, rows), 1) // vec
        == lax.broadcasted_iota(jnp.int32, (pairs, rows), 0)
    ).astype(jnp.bfloat16)
    code_row = jnp.dot(
        jnp.broadcast_to(code, (8, pairs)).astype(jnp.bfloat16),
        spread,
        preferred_element_type=jnp.float32,
    )[0:1, :].astype(jnp.int32)
    x_all = x_ref[...]
    r_it = lax.broadcasted_iota(jnp.int32, (combos, rows), 0)
    c_it = lax.broadcasted_iota(jnp.int32, (combos, rows), 1)
    pack_hot = ((r_it // vec == code_row) & (r_it % vec == c_it % vec)).astype(jnp.bfloat16)
    pick[...] = pack_hot

    chunk = min(combos, 256)
    for at in range(combos // chunk):
        hot = pick[at * chunk : (at + 1) * chunk, :]
        pack[at * chunk : (at + 1) * chunk, :] = jnp.dot(
            hot, x_all, preferred_element_type=jnp.float32
        ).astype(jnp.bfloat16)

    hole = hole_ref[...]
    parts = [
        lax.dot_general(
            hole, occ_ref[i], (((0,), (0,)), ((), ())), preferred_element_type=jnp.float32
        )
        for i in range(bo)
    ]
    fac[...] = jnp.concatenate(parts, axis=0).astype(jnp.bfloat16)

    pl.semaphore_wait(barrier, n - 1 + ns - 1)

    sends = []
    order = list(range(n - 1, 0, -1))
    for j in order:
        to, _ = partner(me, j, n)
        sends.append(copy_to(0, j, pack.at[rows_of(to)], got_a.at[rows_of(me)]))
        sends[-1].start()
    for j in order:
        sends.append(copy_to(1, j, fac, got_f.at[rows_of(me)]))
        sends[-1].start()
    got_a[rows_of(me), :] = pack[rows_of(me), :]
    got_f[rows_of(me), :] = fac[...]

    code_col = jnp.sum(
        jnp.where(
            lax.broadcasted_iota(jnp.int32, (rows, pairs), 0) // vec
            == lax.broadcasted_iota(jnp.int32, (rows, pairs), 1),
            jnp.broadcast_to(code, (rows, pairs)),
            0.0,
        ),
        axis=1,
        keepdims=True,
    ).astype(jnp.int32)
    orb = lax.broadcasted_iota(jnp.int32, (rows, no), 1)
    oe = jnp.broadcast_to(oe_ref[...], (rows, no))

    def energy_of(index):
        return jnp.sum(jnp.where(orb == index, oe, 0.0), axis=1, keepdims=True)

    dest_col = code_col // bo
    first_energy = energy_of(code_col - dest_col * bo + me * bo)
    second = [energy_of(dest_col * bo + m) for m in range(bo)]
    home_hot = (
        (lax.broadcasted_iota(jnp.int32, (rows, combos), 1) // vec == code_col)
        & (
            lax.broadcasted_iota(jnp.int32, (rows, combos), 1) % vec
            == lax.broadcasted_iota(jnp.int32, (rows, combos), 0) % vec
        )
    ).astype(jnp.bfloat16)

    vcopy.wait()
    tile = 256
    tiles = aux // tile
    for j in order:
        copy_to(0, j, pack.at[rows_of(me)], got_a.at[rows_of(partner(me, j, n)[1])]).wait_recv()

    for at in range(combos // chunk):
        here = slice(at * chunk, (at + 1) * chunk)

        def back_tile(t, carry, here=here):
            q = pl.ds(pl.multiple_of(t * tile, tile), tile)
            back[here, q] = lax.dot_general(
                got_a[here, :],
                vir[q, :],
                (((1,), (1,)), ((), ())),
                preferred_element_type=jnp.float32,
            ).astype(jnp.bfloat16)
            return carry

        lax.fori_loop(0, tiles, back_tile, 0)
    for j in order:
        to, _ = partner(me, j, n)
        sends.append(copy_to(2, j, back.at[rows_of(to)], back_home.at[rows_of(me)]))
        sends[-1].start()
    back_home[rows_of(me), :] = back[rows_of(me), :]

    for j in order:
        copy_to(1, j, fac, got_f.at[rows_of(partner(me, j, n)[1])]).wait_recv()
    for at in range(combos // chunk):
        here = slice(at * chunk, (at + 1) * chunk)

        def couple_tile(t, carry, here=here):
            c = pl.ds(pl.multiple_of(t * tile, tile), tile)
            cpl[here, c] = jnp.dot(
                got_f[here, :], vir[:, c], preferred_element_type=jnp.float32
            ).astype(jnp.bfloat16)
            return carry

        lax.fori_loop(0, cols // tile, couple_tile, 0)
    for j in order:
        to, _ = partner(me, j, n)
        sends.append(copy_to(3, j, cpl.at[rows_of(to)], cpl_home.at[rows_of(me)]))
        sends[-1].start()
    cpl_home[rows_of(me), :] = cpl[rows_of(me), :]

    for j in order:
        copy_to(2, j, back.at[rows_of(me)], back_home.at[rows_of(partner(me, j, n)[1])]).wait_recv()
    total = back_home[0:part, :].astype(jnp.float32)
    for d in range(1, n):
        total = total + back_home[d * part : (d + 1) * part, :].astype(jnp.float32)
    local = jnp.zeros((vec, no), jnp.float32)
    for i in range(bo):
        local = local + lax.dot_general(
            total[i * vec : (i + 1) * vec, :],
            occ_ref[i].astype(jnp.float32),
            (((1,), (1,)), ((), ())),
            precision=HIGHEST,
            preferred_element_type=jnp.float32,
        )
    lanes = red.shape[2]
    if lanes > no:
        local = jnp.concatenate([local, jnp.zeros((vec, lanes - no), jnp.float32)], axis=1)
    red[me] = local
    for j in order:
        sends.append(copy_to(4, j, red.at[me], red.at[me]))
        sends[-1].start()
    for j in order:
        copy_to(4, j, red.at[me], red.at[partner(me, j, n)[1]]).wait_recv()
    group = red[0]
    for d in range(1, n):
        group = group + red[d]
    red2[own_z] = group

    def copy_z(j, src, dst):
        return pltpu.make_async_remote_copy(
            src_ref=src,
            dst_ref=dst,
            send_sem=zsend.at[j],
            recv_sem=zrecv.at[j],
            device_id={"sym": partner(own_z, j, ns)[0]},
            device_id_type=MESH,
        )

    for j in range(1, ns):
        sends.append(copy_z(j, red2.at[own_z], red2.at[own_z]))
        sends[-1].start()

    for j in order:
        copy_to(3, j, cpl.at[rows_of(me)], cpl_home.at[rows_of(partner(me, j, n)[1])]).wait_recv()
    ve = ve_ref[...]
    for m in range(bo):
        c = slice(m * virt, (m + 1) * virt)
        coupled = jnp.dot(home_hot, cpl_home[:, c], preferred_element_type=jnp.float32)
        shift = ve - first_energy - second[m]
        out_ref[:, c] = (coupled + shift * x_ref[:, c].astype(jnp.float32)).astype(jnp.bfloat16)

    for j in range(1, ns):
        copy_z(j, red2.at[own_z], red2.at[partner(own_z, j, ns)[1]]).wait_recv()
    whole = red2[0]
    for s in range(1, ns):
        whole = whole + red2[s]
    direct = jnp.dot(
        block_ref[...],
        hole.astype(jnp.float32),
        precision=HIGHEST,
        preferred_element_type=jnp.float32,
    )
    hout_ref[...] = whole.T[0:no, :] + direct
    for copy in sends:
        copy.wait_send()


def body(
    hole_part,
    hole_block,
    amplitudes,
    pair_first,
    pair_block,
    occ_tiles,
    vir_tiles,
    occ_energy,
    vir_energy,
):
    n = lax.axis_size("occ")
    ns = lax.axis_size("sym")
    pairs, vec, bo, virt = amplitudes.shape
    aux = vir_tiles.shape[0]
    no = hole_part.shape[0]
    cols = bo * virt
    rows = pairs * vec
    part = bo * vec
    combos = n * part
    lanes = max(128, no)
    vmem = pl.BlockSpec(memory_space=pltpu.VMEM)
    half = jnp.bfloat16
    sigma, hole = pl.pallas_call(
        functools.partial(kernel, n, ns),
        out_shape=(
            jax.ShapeDtypeStruct((rows, cols), half),
            jax.ShapeDtypeStruct((no, vec), jnp.float32),
        ),
        in_specs=[vmem] * 6 + [pl.BlockSpec(memory_space=pl.ANY)] + [vmem] * 2,
        out_specs=(vmem, vmem),
        scratch_shapes=[
            pltpu.VMEM((aux, cols), half),
            pltpu.VMEM((combos, rows), half),
            pltpu.VMEM((combos, cols), half),
            pltpu.VMEM((part, aux), half),
            pltpu.VMEM((combos, cols), half),
            pltpu.VMEM((combos, aux), half),
            pltpu.VMEM((combos, cols), half),
            pltpu.VMEM((combos, cols), half),
            pltpu.VMEM((combos, aux), half),
            pltpu.VMEM((combos, aux), half),
            pltpu.VMEM((n, vec, lanes), jnp.float32),
            pltpu.VMEM((ns, vec, lanes), jnp.float32),
            pltpu.SemaphoreType.DMA,
            pltpu.SemaphoreType.DMA((5, n)),
            pltpu.SemaphoreType.DMA((5, n)),
            pltpu.SemaphoreType.DMA((ns,)),
            pltpu.SemaphoreType.DMA((ns,)),
        ],
        compiler_params=pltpu.CompilerParams(
            collective_id=0, has_side_effects=True, vmem_limit_bytes=44 * 1024 * 1024
        ),
        cost_estimate=pl.CostEstimate(
            flops=4 * combos * aux * cols, bytes_accessed=2 * aux * cols, transcendentals=0
        ),
    )(
        hole_part,
        hole_block,
        amplitudes.reshape(rows, cols),
        pair_first.reshape(1, pairs),
        pair_block.reshape(1, pairs),
        occ_tiles,
        vir_tiles.reshape(aux, cols),
        occ_energy.reshape(1, no),
        vir_energy.reshape(1, virt),
    )
    return sigma.reshape(amplitudes.shape), hole


def solution(mesh):
    placed = (
        P(),
        P(),
        P(("occ", "sym"), None, None, None),
        P(("occ", "sym")),
        P(("occ", "sym")),
        P("occ", None, None),
        P(None, "occ", None),
        P(),
        P(),
    )
    return jax.shard_map(
        body,
        mesh=mesh,
        in_specs=placed,
        out_specs=(P(("occ", "sym"), None, None, None), P()),
        check_vma=False,
    )
```

time: 118 us -> 41.8 us (0.35)
  blocking collectives: 39.9 us -> 0 us
  Pallas kernels: 0 us -> 34.8 us
  waiting for transfers between devices: 33.7 us -> 0 us
  starting transfers between devices: 17.1 us -> 0 us
  matrix products: 13 us -> 0 us
  other arithmetic: 3.95 us -> 0 us
  local copies, waits for them, and re-layouts: 9.29 us -> 6.01 us
    psum x1 -> x0, blocking collectives: 39.9 us -> none  [body(): hole_total = lax.psum(local_hole, ('occ', 'sym'))]
    pallas_call x0 -> x1, Pallas kernels: none -> 34.8 us  [body(): pl.pallas_call(functools.partial(kernel, n, ns), out_shape=(jax.ShapeDtyp...]
    all_to_all x4 -> x0, waiting for transfers between devices: 33.7 us -> none  [the longest x1 12 us: body(): lax.all_to_all(partial_value, 'occ', split_axis=0, concat_axis=0, tiled=T...]
    all_to_all x4 -> x0, starting transfers between devices: 17.1 us -> none  [the longest x1 5.17 us: body(): lax.all_to_all(slot_factors, 'occ', split_axis=0, concat_axis=0, tiled=True)]
    dot_general x11 -> x0, matrix products: 13 us -> none  [the longest x1 3.74 us: body(): lax.dot_general(got_amp.reshape(slot_count * vectors, columns), vir_flat,...]
    reshape x2 -> x0, local copies, waits for them, and re-layouts: 3.18 us -> none  [the longest x1 2.7 us: body(): vir_flat = vir_tiles.reshape(auxiliary, columns)]
    sub x3 -> x0, other arithmetic: 1.49 us -> none  [the longest x2 0.83 us: body(): vir_energy[None, None, None, :] - first_energy[:, None, None, None]]
    unnamed x20 -> x17, local copies, waits for them, and re-layouts: 5.64 us -> 6.01 us
  transfers between devices with their start and end apart: 4 -> 0, of which waited for: 4 -> 0; matrix products, arithmetic and copies ran while one was open for 15% -> 0% of each run, Pallas kernels for 0% -> 0%
where the time goes in v1:
time: 41.8 us; the launch traced here: 41.6 us
  Pallas kernels  34.8 us (83%)
  local copies, waits for them, and re-layouts  6.01 us (14%)
  between operations  0.75 us (2%)
    pallas_call x1, Pallas kernels, body(): pl.pallas_call(functools.partial(kernel, n, ns), out_shape=(jax.ShapeDtyp...  34.8 us
    unnamed x17, local copies, waits for them, and re-layouts  6.01 us

profile of v1, /device:TPU:0, one launch (start us, length us, event | category | flops | bytes accessed | tf_op | source)
XLA Modules:
  0.0 41.6 jit_solution(17524489706703720722)
XLA Ops:
  0.6 0.8 %copy.11.hole_ref = bf16[32,8]{1,0:T(8,128)(2,1)S(1)} copy(bf16[32,8]{0,1:T(8,128)(2,1)} %param.9) | data formatting | bytes 1024 | tf_op args[0]
  1.4 1.2 %copy.14 = bf16[40,8,4,256]{3,1,2,0:T(8,128)(2,1)S(1)} copy(bf16[40,8,4,256]{3,2,1,0:T(4,128)(2,1)} %param.11) | data formatting | bytes 1310720
  2.6 0.0 copy-start
  2.6 0.0 copy-start.1
  2.6 0.0 copy-start.2
  2.6 0.0 copy-start.3
  2.7 0.0 copy-start.4
  2.7 0.0 copy-start.5
  2.7 2.2 %copy.15 = bf16[128,8,4,256]{3,1,2,0:T(8,128)(2,1)S(1)} copy(bf16[128,8,4,256]{3,2,1,0:T(4,128)(2,1)} %bitcast.17) | data formatting | bytes 4194304
  4.9 0.0 copy-done
  4.9 0.0 copy-done.1
  4.9 0.0 copy-done.2
  4.9 0.0 copy-done.3
  4.9 0.0 copy-done.4
  4.9 0.0 copy-done.5
  4.9 34.8 %shard_map.104 = (bf16[320,1024]{1,0:T(8,128)(2,1)S(1)}, f32[32,8]{1,0:T(8,128)S(1)}) custom-call(bf16[32,8]{1,0:T(8,128)(2,1)S(1)} %copy.11.hole_ref, f32[32,32]{1,0:T(8,128)S(1)} %copy-done.1, bf16[320,1024]{1,0:T(8,128)(2,1)S(1)} %bitcast.12, s32[1,40]{1,0:T(1,128)S(1)} %bitcast.14, s32[1,40]{1,0:T(1,128)S(1)} %bitcast.15, ...), custom_call_target="tpu_custom_call" | custom-call | flops 1073741824 | bytes 2097152 | tf_op jit(solution)/shard_map/pallas_call | solution.py:299
  39.8 1.2 %copy.12 = bf16[40,8,4,256]{3,2,1,0:T(4,128)(2,1)} copy(bf16[40,8,4,256]{3,1,2,0:T(8,128)(2,1)S(1)} %bitcast.11) | data formatting | bytes 1310720
  40.9 0.7 %copy.13 = f32[32,8]{0,1:T(8,128)} copy(f32[32,8]{1,0:T(8,128)S(1)} %get-tuple-element.7) | data formatting | bytes 2048
Async XLA Ops:
  2.6 2.3 %copy-start = (bf16[4,32,1024]{2,1,0:T(8,128)(2,1)S(1)}, bf16[4,32,1024]{2,1,0:T(8,128)(2,1)}, u32[]{:S(2)}) copy-start(bf16[4,32,1024]{2,1,0:T(8,128)(2,1)} %occ_ref.1) | copy-start | bytes 786436
  2.6 2.2 %copy-start.1 = (f32[32,32]{1,0:T(8,128)S(1)}, f32[32,32]{1,0:T(8,128)}, u32[]{:S(2)}) copy-start(f32[32,32]{1,0:T(8,128)} %block_ref.1) | copy-start | bytes 12292
  2.6 2.2 %copy-start.2 = (f32[256]{0:T(256)S(1)}, f32[256]{0:T(256)}, u32[]{:S(2)}) copy-start(f32[256]{0:T(256)} %param.17) | copy-start | bytes 3076
  2.6 2.2 %copy-start.3 = (s32[40]{0:T(128)S(1)}, s32[40]{0:T(128)}, u32[]{:S(2)}) copy-start(s32[40]{0:T(128)} %param.12) | copy-start | bytes 484
  2.7 2.2 %copy-start.4 = (s32[40]{0:T(128)S(1)}, s32[40]{0:T(128)}, u32[]{:S(2)}) copy-start(s32[40]{0:T(128)} %param.13) | copy-start | bytes 484
  2.7 2.2 %copy-start.5 = (f32[32]{0:T(128)S(1)}, f32[32]{0:T(128)}, u32[]{:S(2)}) copy-start(f32[32]{0:T(128)} %param.16) | copy-start | bytes 388

commit v2 on v1

--- a/solution.py
+++ b/solution.py
@@ -37,6 +37,8 @@
     ve_ref,
     out_ref,
     hout_ref,
+    vir_raw,
+    wide,
     vir,
     pick,
     pack,
@@ -58,7 +60,7 @@
     me = lax.axis_index("occ")
     own_z = lax.axis_index("sym")
     bo, no, aux = occ_ref.shape
-    vec = hole_ref.shape[1]
+    vec = hole_ref.shape[0]
     rows, cols = x_ref.shape
     virt = ve_ref.shape[1]
     pairs = first_ref.shape[1]
@@ -72,7 +74,7 @@
         pl.semaphore_signal(
             barrier, 1, device_id={"sym": partner(own_z, j, ns)[0]}, device_id_type=MESH
         )
-    vcopy = pltpu.make_async_copy(vir_hbm, vir, vsem)
+    vcopy = pltpu.make_async_copy(vir_hbm, vir_raw, vsem)
     vcopy.start()
 
     def rows_of(index):
@@ -90,7 +92,7 @@
 
     code = (dest_ref[...] * bo + first_ref[...] - me * bo).astype(jnp.float32)
     spread = (
-        lax.broadcasted_iota(jnp.int32, (pairs, rows), 1) // vec
+        lax.broadcasted_iota(jnp.int32, (1, rows), 1) // vec
         == lax.broadcasted_iota(jnp.int32, (pairs, rows), 0)
     ).astype(jnp.bfloat16)
     code_row = jnp.dot(
@@ -99,9 +101,8 @@
         preferred_element_type=jnp.float32,
     )[0:1, :].astype(jnp.int32)
     x_all = x_ref[...]
-    r_it = lax.broadcasted_iota(jnp.int32, (combos, rows), 0)
-    c_it = lax.broadcasted_iota(jnp.int32, (combos, rows), 1)
-    pack_hot = ((r_it // vec == code_row) & (r_it % vec == c_it % vec)).astype(jnp.bfloat16)
+    col_key = code_row * vec + lax.broadcasted_iota(jnp.int32, (1, rows), 1) % vec
+    pack_hot = (lax.broadcasted_iota(jnp.int32, (combos, rows), 0) == col_key).astype(jnp.bfloat16)
     pick[...] = pack_hot
 
     chunk = min(combos, 256)
@@ -113,10 +114,7 @@
 
     hole = hole_ref[...]
     parts = [
-        lax.dot_general(
-            hole, occ_ref[i], (((0,), (0,)), ((), ())), preferred_element_type=jnp.float32
-        )
-        for i in range(bo)
+        jnp.dot(hole, occ_ref[i], preferred_element_type=jnp.float32) for i in range(bo)
     ]
     fac[...] = jnp.concatenate(parts, axis=0).astype(jnp.bfloat16)
 
@@ -136,7 +134,7 @@
 
     code_col = jnp.sum(
         jnp.where(
-            lax.broadcasted_iota(jnp.int32, (rows, pairs), 0) // vec
+            lax.broadcasted_iota(jnp.int32, (rows, 1), 0) // vec
             == lax.broadcasted_iota(jnp.int32, (rows, pairs), 1),
             jnp.broadcast_to(code, (rows, pairs)),
             0.0,
@@ -153,15 +151,29 @@
     dest_col = code_col // bo
     first_energy = energy_of(code_col - dest_col * bo + me * bo)
     second = [energy_of(dest_col * bo + m) for m in range(bo)]
-    home_hot = (
-        (lax.broadcasted_iota(jnp.int32, (rows, combos), 1) // vec == code_col)
-        & (
-            lax.broadcasted_iota(jnp.int32, (rows, combos), 1) % vec
-            == lax.broadcasted_iota(jnp.int32, (rows, combos), 0) % vec
-        )
-    ).astype(jnp.bfloat16)
+    row_key = code_col * vec + lax.broadcasted_iota(jnp.int32, (rows, 1), 0) % vec
+    home_hot = (lax.broadcasted_iota(jnp.int32, (rows, combos), 1) == row_key).astype(jnp.bfloat16)
 
     vcopy.wait()
+    step = vir_raw.shape[0] // aux
+    halves = step // bo
+    lane = vir_raw.shape[1]
+    some = wide.shape[1] // step
+
+    def spread_rows(block, carry):
+        slot = block % 2
+        wide[slot] = vir_raw[
+            pl.ds(pl.multiple_of(block * some * step, some * step), some * step), :
+        ].astype(jnp.float32)
+        here = pl.ds(pl.multiple_of(block * some, some), some)
+        for t in range(halves):
+            for m in range(bo):
+                vir[here, m * virt + t * lane : m * virt + (t + 1) * lane] = wide[
+                    slot, pl.ds(t * bo + m, some, stride=step), :
+                ].astype(jnp.bfloat16)
+        return carry
+
+    lax.fori_loop(0, aux // some, spread_rows, 0)
     tile = 256
     tiles = aux // tile
     for j in order:
@@ -262,13 +274,14 @@
     whole = red2[0]
     for s in range(1, ns):
         whole = whole + red2[s]
-    direct = jnp.dot(
+    direct = lax.dot_general(
+        hole.astype(jnp.float32),
         block_ref[...],
-        hole.astype(jnp.float32),
+        (((1,), (1,)), ((), ())),
         precision=HIGHEST,
         preferred_element_type=jnp.float32,
     )
-    hout_ref[...] = whole.T[0:no, :] + direct
+    hout_ref[...] = whole[:, 0:no] + direct
     for copy in sends:
         copy.wait_send()
 
@@ -300,11 +313,13 @@
         functools.partial(kernel, n, ns),
         out_shape=(
             jax.ShapeDtypeStruct((rows, cols), half),
-            jax.ShapeDtypeStruct((no, vec), jnp.float32),
+            jax.ShapeDtypeStruct((vec, no), jnp.float32),
         ),
         in_specs=[vmem] * 6 + [pl.BlockSpec(memory_space=pl.ANY)] + [vmem] * 2,
         out_specs=(vmem, vmem),
         scratch_shapes=[
+            pltpu.VMEM((aux * cols // 128, 128), half),
+            pltpu.VMEM((2, 64 * cols // 128, 128), jnp.float32),
             pltpu.VMEM((aux, cols), half),
             pltpu.VMEM((combos, rows), half),
             pltpu.VMEM((combos, cols), half),
@@ -330,17 +345,19 @@
             flops=4 * combos * aux * cols, bytes_accessed=2 * aux * cols, transcendentals=0
         ),
     )(
-        hole_part,
+        hole_part.T,
         hole_block,
         amplitudes.reshape(rows, cols),
         pair_first.reshape(1, pairs),
         pair_block.reshape(1, pairs),
         occ_tiles,
-        vir_tiles.reshape(aux, cols),
+        vir_tiles.reshape(aux, bo, virt // 128, 128)
+        .transpose(0, 2, 1, 3)
+        .reshape(aux * cols // 128, 128),
         occ_energy.reshape(1, no),
         vir_energy.reshape(1, virt),
     )
-    return sigma.reshape(amplitudes.shape), hole
+    return sigma.reshape(amplitudes.shape), hole.T
 
 
 def solution(mesh):

time: 41.8 us -> 45.3 us (1.084)
  local copies, waits for them, and re-layouts: 6.01 us -> 9.54 us
    unnamed x17 -> x19, local copies, waits for them, and re-layouts: 6.01 us -> 9.54 us
where the time goes in v2:
time: 45.3 us; the launch traced here: 45 us
  Pallas kernels  34.8 us (77%)
  local copies, waits for them, and re-layouts  9.54 us (21%)
  between operations  0.66 us (1%)
    pallas_call x1, Pallas kernels, body(): pl.pallas_call(functools.partial(kernel, n, ns), out_shape=(jax.ShapeDtyp...  34.8 us
    unnamed x19, local copies, waits for them, and re-layouts  9.54 us

profile of v2, /device:TPU:0, one launch (start us, length us, event | category | flops | bytes accessed | tf_op | source)
XLA Modules:
  0.0 45.0 jit_solution(11163475985905039546)
XLA Ops:
  0.6 1.2 %copy.13 = bf16[40,8,4,256]{3,1,2,0:T(8,128)(2,1)S(1)} copy(bf16[40,8,4,256]{3,2,1,0:T(4,128)(2,1)} %param.11) | data formatting | bytes 1310720
  1.8 0.0 copy-start
  1.9 1.6 %copy-done = bf16[1024,4,256]{2,1,0:T(4,128)(2,1)S(1)} copy-done((bf16[1024,4,256]{2,1,0:T(4,128)(2,1)S(1)}, bf16[1024,4,256]{2,1,0:T(4,128)(2,1)}, u32[]{:S(2)}) %copy-start) | copy-done | bytes 2097176
  3.4 0.0 copy-start.1
  3.4 0.9 %copy-done.1 = bf16[4,32,1024]{2,1,0:T(8,128)(2,1)S(1)} copy-done((bf16[4,32,1024]{2,1,0:T(8,128)(2,1)S(1)}, bf16[4,32,1024]{2,1,0:T(8,128)(2,1)}, u32[]{:S(2)}) %copy-start.1) | copy-done | bytes 262168
  4.4 0.0 copy-start.2
  4.4 0.7 %copy-done.2 = f32[32,32]{1,0:T(8,128)S(1)} copy-done((f32[32,32]{1,0:T(8,128)S(1)}, f32[32,32]{1,0:T(8,128)}, u32[]{:S(2)}) %copy-start.2) | copy-done | bytes 4120
  5.1 0.0 copy-start.3
  5.1 0.7 %copy-done.3 = bf16[32,8]{0,1:T(8,128)(2,1)S(1)} copy-done((bf16[32,8]{0,1:T(8,128)(2,1)S(1)}, bf16[32,8]{0,1:T(8,128)(2,1)}, u32[]{:S(2)}) %copy-start.3) | copy-done | bytes 536
  5.8 0.0 copy-start.4
  5.8 0.7 %copy-done.4 = f32[256]{0:T(256)S(1)} copy-done((f32[256]{0:T(256)S(1)}, f32[256]{0:T(256)}, u32[]{:S(2)}) %copy-start.4) | copy-done | bytes 1048
  6.5 0.0 copy-start.5
  6.5 0.7 %copy-done.5 = s32[40]{0:T(128)S(1)} copy-done((s32[40]{0:T(128)S(1)}, s32[40]{0:T(128)}, u32[]{:S(2)}) %copy-start.5) | copy-done | bytes 184
  7.1 0.0 copy-start.6
  7.1 0.7 %copy-done.6 = s32[40]{0:T(128)S(1)} copy-done((s32[40]{0:T(128)S(1)}, s32[40]{0:T(128)}, u32[]{:S(2)}) %copy-start.6) | copy-done | bytes 184
  7.8 0.0 copy-start.7
  7.8 0.7 %copy-done.7 = f32[32]{0:T(128)S(1)} copy-done((f32[32]{0:T(128)S(1)}, f32[32]{0:T(128)}, u32[]{:S(2)}) %copy-start.7) | copy-done | bytes 152
  8.4 34.8 %shard_map.104 = (bf16[320,1024]{1,0:T(8,128)(2,1)S(1)}, f32[8,32]{1,0:T(8,128)S(1)}) custom-call(bf16[8,32]{1,0:T(8,128)(2,1)S(1)} %bitcast.19, f32[32,32]{1,0:T(8,128)S(1)} %copy-done.2, bf16[320,1024]{1,0:T(8,128)(2,1)S(1)} %bitcast.16, s32[1,40]{1,0:T(1,128)S(1)} %bitcast.21, s32[1,40]{1,0:T(1,128)S(1)} %bitcast.22, bf16[4,32,1024]{2,1,0:T(8,128)(2,1)S(1)} %copy-done.1, ...), custom_call_target="tpu_custom_call" | custom-call | flops 1073741824 | bytes 2097152 | tf_op jit(solution)/shard_map/pallas_call | solution.py:312
  43.2 1.2 %copy.12 = bf16[40,8,4,256]{3,2,1,0:T(4,128)(2,1)} copy(bf16[40,8,4,256]{3,1,2,0:T(8,128)(2,1)S(1)} %bitcast.15) | data formatting | bytes 1310720
  44.4 0.6 %copy.15 = f32[32,8]{0,1:T(8,128)} copy(f32[32,8]{0,1:T(8,128)S(1)} %bitcast.17) | data formatting | bytes 2048
Async XLA Ops:
  1.8 1.6 %copy-start = (bf16[1024,4,256]{2,1,0:T(4,128)(2,1)S(1)}, bf16[1024,4,256]{2,1,0:T(4,128)(2,1)}, u32[]{:S(2)}) copy-start(bf16[1024,4,256]{2,1,0:T(4,128)(2,1)} %param.15) | copy-start | bytes 6291460
  3.4 0.9 %copy-start.1 = (bf16[4,32,1024]{2,1,0:T(8,128)(2,1)S(1)}, bf16[4,32,1024]{2,1,0:T(8,128)(2,1)}, u32[]{:S(2)}) copy-start(bf16[4,32,1024]{2,1,0:T(8,128)(2,1)} %occ_ref.1) | copy-start | bytes 786436
  4.4 0.7 %copy-start.2 = (f32[32,32]{1,0:T(8,128)S(1)}, f32[32,32]{1,0:T(8,128)}, u32[]{:S(2)}) copy-start(f32[32,32]{1,0:T(8,128)} %block_ref.1) | copy-start | bytes 12292
  5.1 0.7 %copy-start.3 = (bf16[32,8]{0,1:T(8,128)(2,1)S(1)}, bf16[32,8]{0,1:T(8,128)(2,1)}, u32[]{:S(2)}) copy-start(bf16[32,8]{0,1:T(8,128)(2,1)} %param.9) | copy-start | bytes 1540
  5.8 0.7 %copy-start.4 = (f32[256]{0:T(256)S(1)}, f32[256]{0:T(256)}, u32[]{:S(2)}) copy-start(f32[256]{0:T(256)} %param.17) | copy-start | bytes 3076
  6.5 0.7 %copy-start.5 = (s32[40]{0:T(128)S(1)}, s32[40]{0:T(128)}, u32[]{:S(2)}) copy-start(s32[40]{0:T(128)} %param.12) | copy-start | bytes 484
  7.1 0.7 %copy-start.6 = (s32[40]{0:T(128)S(1)}, s32[40]{0:T(128)}, u32[]{:S(2)}) copy-start(s32[40]{0:T(128)} %param.13) | copy-start | bytes 484
  7.8 0.7 %copy-start.7 = (f32[32]{0:T(128)S(1)}, f32[32]{0:T(128)}, u32[]{:S(2)}) copy-start(f32[32]{0:T(128)} %param.16) | copy-start | bytes 388

commit v3 on v2

--- a/solution.py
+++ b/solution.py
@@ -26,17 +26,25 @@
 def kernel(
     n,
     ns,
+    hole_hbm,
+    block_hbm,
+    x_ref,
+    first_hbm,
+    dest_hbm,
+    occ_hbm,
+    vir_hbm,
+    oe_hbm,
+    ve_hbm,
+    out_ref,
+    hout_ref,
     hole_ref,
     block_ref,
-    x_ref,
     first_ref,
     dest_ref,
     occ_ref,
-    vir_hbm,
     oe_ref,
     ve_ref,
-    out_ref,
-    hout_ref,
+    load_sem,
     vir_raw,
     wide,
     vir,
@@ -56,6 +64,8 @@
     recv_sem,
     zsend,
     zrecv,
+    zcsend,
+    zcrecv,
 ):
     me = lax.axis_index("occ")
     own_z = lax.axis_index("sym")
@@ -66,6 +76,9 @@
     pairs = first_ref.shape[1]
     part = bo * vec
     combos = n * part
+    half = part // 2
+    side = own_z % 2
+    other_side = 1 - side
 
     barrier = pltpu.get_barrier_semaphore()
     for j in range(1, n):
@@ -75,10 +88,31 @@
             barrier, 1, device_id={"sym": partner(own_z, j, ns)[0]}, device_id_type=MESH
         )
     vcopy = pltpu.make_async_copy(vir_hbm, vir_raw, vsem)
+    loads = [
+        pltpu.make_async_copy(src, dst, load_sem.at[at])
+        for at, (src, dst) in enumerate(
+            [
+                (first_hbm, first_ref),
+                (dest_hbm, dest_ref),
+                (hole_hbm, hole_ref),
+                (occ_hbm, occ_ref),
+                (oe_hbm, oe_ref),
+                (ve_hbm, ve_ref),
+                (block_hbm, block_ref),
+            ]
+        )
+    ]
+    for load in loads:
+        load.start()
     vcopy.start()
+    loads[0].wait()
+    loads[1].wait()
 
     def rows_of(index):
         return pl.ds(pl.multiple_of(index * part, part), part)
+
+    def half_of(index):
+        return pl.ds(pl.multiple_of(index * half, half), half)
 
     def copy_to(kind, j, src, dst):
         return pltpu.make_async_remote_copy(
@@ -112,6 +146,8 @@
             hot, x_all, preferred_element_type=jnp.float32
         ).astype(jnp.bfloat16)
 
+    loads[2].wait()
+    loads[3].wait()
     hole = hole_ref[...]
     parts = [
         jnp.dot(hole, occ_ref[i], preferred_element_type=jnp.float32) for i in range(bo)
@@ -127,10 +163,10 @@
         sends.append(copy_to(0, j, pack.at[rows_of(to)], got_a.at[rows_of(me)]))
         sends[-1].start()
     for j in order:
-        sends.append(copy_to(1, j, fac, got_f.at[rows_of(me)]))
+        sends.append(copy_to(1, j, fac.at[half_of(side)], got_f.at[half_of(me)]))
         sends[-1].start()
     got_a[rows_of(me), :] = pack[rows_of(me), :]
-    got_f[rows_of(me), :] = fac[...]
+    got_f[half_of(me), :] = fac[half_of(side), :]
 
     code_col = jnp.sum(
         jnp.where(
@@ -142,6 +178,8 @@
         axis=1,
         keepdims=True,
     ).astype(jnp.int32)
+    for load in loads[4:]:
+        load.wait()
     orb = lax.broadcasted_iota(jnp.int32, (rows, no), 1)
     oe = jnp.broadcast_to(oe_ref[...], (rows, no))
 
@@ -200,9 +238,11 @@
     back_home[rows_of(me), :] = back[rows_of(me), :]
 
     for j in order:
-        copy_to(1, j, fac, got_f.at[rows_of(partner(me, j, n)[1])]).wait_recv()
-    for at in range(combos // chunk):
-        here = slice(at * chunk, (at + 1) * chunk)
+        source = partner(me, j, n)[1]
+        copy_to(1, j, fac.at[half_of(side)], got_f.at[half_of(source)]).wait_recv()
+    thin = min(n * half, 256)
+    for at in range(n * half // thin):
+        here = slice(at * thin, (at + 1) * thin)
 
         def couple_tile(t, carry, here=here):
             c = pl.ds(pl.multiple_of(t * tile, tile), tile)
@@ -214,9 +254,22 @@
         lax.fori_loop(0, cols // tile, couple_tile, 0)
     for j in order:
         to, _ = partner(me, j, n)
-        sends.append(copy_to(3, j, cpl.at[rows_of(to)], cpl_home.at[rows_of(me)]))
-        sends[-1].start()
-    cpl_home[rows_of(me), :] = cpl[rows_of(me), :]
+        sends.append(copy_to(3, j, cpl.at[half_of(to)], cpl_home.at[half_of(me * 2 + side)]))
+        sends[-1].start()
+    cpl_home[half_of(me * 2 + side), :] = cpl[half_of(me), :]
+
+    def pass_on(j, rows):
+        return pltpu.make_async_remote_copy(
+            src_ref=cpl_home.at[rows],
+            dst_ref=cpl_home.at[rows],
+            send_sem=zcsend.at[j],
+            recv_sem=zcrecv.at[j],
+            device_id={"sym": own_z + 1 - 2 * side},
+            device_id_type=MESH,
+        )
+
+    sends.append(pass_on(0, half_of(me * 2 + side)))
+    sends[-1].start()
 
     for j in order:
         copy_to(2, j, back.at[rows_of(me)], back_home.at[rows_of(partner(me, j, n)[1])]).wait_recv()
@@ -240,6 +293,12 @@
         sends.append(copy_to(4, j, red.at[me], red.at[me]))
         sends[-1].start()
     for j in order:
+        rows_in = half_of(partner(me, j, n)[1] * 2 + side)
+        copy_to(3, j, cpl.at[half_of(me)], cpl_home.at[rows_in]).wait_recv()
+        sends.append(pass_on(j, rows_in))
+        sends[-1].start()
+
+    for j in order:
         copy_to(4, j, red.at[me], red.at[partner(me, j, n)[1]]).wait_recv()
     group = red[0]
     for d in range(1, n):
@@ -260,8 +319,9 @@
         sends.append(copy_z(j, red2.at[own_z], red2.at[own_z]))
         sends[-1].start()
 
-    for j in order:
-        copy_to(3, j, cpl.at[rows_of(me)], cpl_home.at[rows_of(partner(me, j, n)[1])]).wait_recv()
+    pass_on(0, half_of(me * 2 + other_side)).wait_recv()
+    for j in order:
+        pass_on(j, half_of(partner(me, j, n)[1] * 2 + other_side)).wait_recv()
     ve = ve_ref[...]
     for m in range(bo):
         c = slice(m * virt, (m + 1) * virt)
@@ -308,6 +368,7 @@
     combos = n * part
     lanes = max(128, no)
     vmem = pl.BlockSpec(memory_space=pltpu.VMEM)
+    anywhere = pl.BlockSpec(memory_space=pl.ANY)
     half = jnp.bfloat16
     sigma, hole = pl.pallas_call(
         functools.partial(kernel, n, ns),
@@ -315,9 +376,17 @@
             jax.ShapeDtypeStruct((rows, cols), half),
             jax.ShapeDtypeStruct((vec, no), jnp.float32),
         ),
-        in_specs=[vmem] * 6 + [pl.BlockSpec(memory_space=pl.ANY)] + [vmem] * 2,
+        in_specs=[anywhere] * 2 + [vmem] + [anywhere] * 6,
         out_specs=(vmem, vmem),
         scratch_shapes=[
+            pltpu.VMEM((vec, no), half),
+            pltpu.VMEM((no, no), jnp.float32),
+            pltpu.VMEM((1, pairs), jnp.int32),
+            pltpu.VMEM((1, pairs), jnp.int32),
+            pltpu.VMEM((bo, no, aux), half),
+            pltpu.VMEM((1, no), jnp.float32),
+            pltpu.VMEM((1, virt), jnp.float32),
+            pltpu.SemaphoreType.DMA((7,)),
             pltpu.VMEM((aux * cols // 128, 128), half),
             pltpu.VMEM((2, 64 * cols // 128, 128), jnp.float32),
             pltpu.VMEM((aux, cols), half),
@@ -325,8 +394,8 @@
             pltpu.VMEM((combos, cols), half),
             pltpu.VMEM((part, aux), half),
             pltpu.VMEM((combos, cols), half),
-            pltpu.VMEM((combos, aux), half),
-            pltpu.VMEM((combos, cols), half),
+            pltpu.VMEM((combos // 2, aux), half),
+            pltpu.VMEM((combos // 2, cols), half),
             pltpu.VMEM((combos, cols), half),
             pltpu.VMEM((combos, aux), half),
             pltpu.VMEM((combos, aux), half),
@@ -337,9 +406,11 @@
             pltpu.SemaphoreType.DMA((5, n)),
             pltpu.SemaphoreType.DMA((ns,)),
             pltpu.SemaphoreType.DMA((ns,)),
+            pltpu.SemaphoreType.DMA((n,)),
+            pltpu.SemaphoreType.DMA((n,)),
         ],
         compiler_params=pltpu.CompilerParams(
-            collective_id=0, has_side_effects=True, vmem_limit_bytes=44 * 1024 * 1024
+            collective_id=0, has_side_effects=True, vmem_limit_bytes=60 * 1024 * 1024
         ),
         cost_estimate=pl.CostEstimate(
             flops=4 * combos * aux * cols, bytes_accessed=2 * aux * cols, transcendentals=0

time: 45.3 us -> 41.1 us (0.907)
  local copies, waits for them, and re-layouts: 9.54 us -> 5.58 us
    unnamed x19 -> x3, local copies, waits for them, and re-layouts: 9.54 us -> 5.58 us
where the time goes in v3:
time: 41.1 us; the launch traced here: 40.8 us
  Pallas kernels  34.6 us (84%)
  local copies, waits for them, and re-layouts  5.58 us (14%)
  between operations  0.64 us (2%)
    pallas_call x1, Pallas kernels, body(): pl.pallas_call(functools.partial(kernel, n, ns), out_shape=(jax.ShapeDtyp...  34.6 us
    unnamed x3, local copies, waits for them, and re-layouts  5.58 us

profile of v3, /device:TPU:0, one launch (start us, length us, event | category | flops | bytes accessed | tf_op | source)
XLA Modules:
  0.0 40.8 jit_solution(11383315783151300786)
XLA Ops:
  0.6 2.1 %copy.13 = bf16[40,8,4,256]{3,1,2,0:T(8,128)(2,1)} copy(bf16[40,8,4,256]{3,2,1,0:T(4,128)(2,1)} %param.11) | data formatting | bytes 1310720
  2.7 34.6 %shard_map.104 = (bf16[320,1024]{1,0:T(8,128)(2,1)}, f32[8,32]{1,0:T(8,128)}) custom-call(bf16[8,32]{1,0:T(8,128)(2,1)} %bitcast.19, f32[32,32]{1,0:T(8,128)} %block_hbm.1, bf16[320,1024]{1,0:T(8,128)(2,1)} %bitcast.16, s32[1,40]{1,0:T(1,128)} %bitcast.21, s32[1,40]{1,0:T(1,128)} %bitcast.22, bf16[4,32,1024]{2,1,0:T(8,128)(2,1)} %occ_hbm.1, ...), custom_call_target="tpu_custom_call" | custom-call | flops 1073741824 | bytes 2097152 | tf_op jit(solution)/shard_map/pallas_call | solution.py:373
  37.3 2.2 %copy.12 = bf16[40,8,4,256]{3,2,1,0:T(4,128)(2,1)} copy(bf16[40,8,4,256]{3,1,2,0:T(8,128)(2,1)} %bitcast.15) | data formatting | bytes 1310720
  39.5 1.3 %copy.15 = f32[32,8]{0,1:T(8,128)} copy(f32[32,8]{0,1:T(8,128)} %bitcast.17) | data formatting | bytes 2048
